TPU v7x, 128 devices: a whole 4x4x4 slice. The times are simulated.
128 devices in a mesh: dp: 32 (over x_hi, y, z), feat: 4 (over x_lo, core).
Axes of the slice: x: 4 (x_hi: 2, x_lo: 2; x = x_hi * 2 + x_lo), y: 4, z: 4, core: 2. Of those that a mesh axis runs over, the one named last changes fastest.
Arguments:
- view_a: bfloat16 [24576, 4096], P('dp', 'feat'), may hold values from -4000 to 4000, as said below
- view_b: bfloat16 [24576, 4096], P('dp', 'feat'), may hold values from -4000 to 4000, as said below
Outputs:
- loss: float32 [], replicated
- grad_a: bfloat16 [24576, 4096], P('dp', 'feat')
- grad_b: bfloat16 [24576, 4096], P('dp', 'feat')
Inputs may be any that keep to these rules, and one draw needn't show every extreme that they name: `view_a`: for every feature, the magnitude of its mean over all 24576 samples is at most 20 times its standard deviation over them, and that standard deviation is 0.5 or more. `view_b`: for every feature, the magnitude of its mean over all 24576 samples is at most 20 times its standard deviation over them, and that standard deviation is 0.5 or more.
All inputs are finite; a program needn't handle non-finite values.
Results may differ from a plain program's by a relative error of at most 0.0039.
Values may be sent and summed in bfloat16 or wider, within the bound.
No kernel may reach another device: no remote copies, remote signals or barrier semaphores. Data moves between devices by JAX's collectives and lax.ppermute only.
A program may use at most 128 MiB of HBM per device.

v0:
```python
import jax
import jax.numpy as jnp
from jax import lax
from jax.sharding import PartitionSpec as P

epsilon = 1e-05
off_weight = 0.0051


def backward(upstream, normed, inverse, sum_up, sum_cross, pairs):
    return (inverse * (upstream - sum_up / pairs - normed * (sum_cross / pairs))).astype(
        jnp.bfloat16
    )


def on_device(view_a, view_b):
    dp_count = lax.axis_size("dp")
    feat_count = lax.axis_size("feat")
    rows, width = view_a.shape
    pairs = rows * dp_count
    full_width = width * feat_count
    first = view_a.astype(jnp.float32)
    second = view_b.astype(jnp.float32)
    sum_first, sum_second = lax.psum((jnp.sum(first, axis=0), jnp.sum(second, axis=0)), "dp")
    centred_a = first - sum_first / pairs
    centred_b = second - sum_second / pairs
    square_a, square_b = lax.psum(
        (jnp.sum(centred_a * centred_a, axis=0), jnp.sum(centred_b * centred_b, axis=0)), "dp"
    )
    var_a = square_a / pairs
    var_b = square_b / pairs
    inv_a = lax.rsqrt(var_a + epsilon)
    inv_b = lax.rsqrt(var_b + epsilon)
    norm_a = centred_a * inv_a
    norm_b = centred_b * inv_b
    low_a = norm_a.astype(jnp.bfloat16)
    low_b = norm_b.astype(jnp.bfloat16)
    second_full = lax.all_gather(low_b, "feat", axis=1, tiled=True)
    dp_index = lax.axis_index("dp")
    feat_index = lax.axis_index("feat")
    keep = width // dp_count
    row_ids = feat_index * width + dp_index * keep + jnp.arange(keep, dtype=jnp.int32)
    col_ids = jnp.arange(full_width, dtype=jnp.int32)
    corr_tile = (
        lax.psum_scatter(
            lax.dot_general(
                low_a, second_full, (((0,), (0,)), ((), ())), preferred_element_type=jnp.float32
            ),
            "dp",
            scatter_dimension=0,
            tiled=True,
        )
        / pairs
    )
    on_diagonal = row_ids[:, None] == col_ids[None, :]
    partial_value = jnp.sum(
        jnp.where(
            on_diagonal, (1.0 - corr_tile) * (1.0 - corr_tile), off_weight * corr_tile * corr_tile
        )
    )
    loss = lax.psum(partial_value, ("dp", "feat"))
    slope = jnp.where(on_diagonal, -2.0 * (1.0 - corr_tile), 2.0 * off_weight * corr_tile).astype(
        jnp.bfloat16
    )
    gathered = lax.all_gather(slope, "dp", axis=0, tiled=True)
    up_a = lax.dot_general(
        second_full, gathered, (((1,), (1,)), ((), ())), preferred_element_type=jnp.float32
    )
    part_b = jnp.dot(low_a, gathered, preferred_element_type=jnp.float32)
    up_b = lax.psum_scatter(part_b, "feat", scatter_dimension=1, tiled=True)
    sum_up_a, cross_a, sum_up_b, cross_b = lax.psum(
        (
            jnp.sum(up_a, axis=0),
            jnp.sum(up_a * norm_a, axis=0),
            jnp.sum(up_b, axis=0),
            jnp.sum(up_b * norm_b, axis=0),
        ),
        "dp",
    )
    grad_a = backward(up_a, norm_a, inv_a, sum_up_a, cross_a, pairs)
    grad_b = backward(up_b, norm_b, inv_b, sum_up_b, cross_b, pairs)
    return (loss, grad_a, grad_b)


def solution(mesh):
    in_specs = (P("dp", "feat"), P("dp", "feat"))
    out_specs = (P(), P("dp", "feat"), P("dp", "feat"))
    return jax.shard_map(
        on_device, mesh=mesh, in_specs=in_specs, out_specs=out_specs, check_vma=False
    )
```

profile of v0, /device:TPU:0, one launch (start us, length us, event | category | flops | bytes accessed | tf_op | source)
XLA Modules:
  0.0 929.1 jit_solution(3711676328444292066)
XLA Ops:
  7.2 0.0 all-gather.3.cloned.1.call-start
  7.2 1.8 convert_reduce_fusion
  9.1 1.7 convert_reduce_fusion.1
  10.7 99.0 %all-reduce.2 = (f32[1024]{0:T(1024)S(1)}, f32[1024]{0:T(1024)S(1)}) all-reduce(f32[1024]{0:T(1024)S(1)} %convert_reduce_fusion, f32[1024]{0:T(1024)S(1)} %convert_reduce_fusion.1), channel_id=1, replica_groups=mesh['dp'=32,'feat'=4] {'dp'}, use_global_device_ids=true, to_apply=%region_5.0 | all-reduce | flops 2048 | bytes 16384 | tf_op jit(solution)/shard_map/psum | solution.py:24
  109.8 0.5 fusion.14
  110.3 0.5 fusion.19
  110.7 89.9 %all-reduce.1 = (f32[1024]{0:T(1024)S(1)}, f32[1024]{0:T(1024)S(1)}) all-reduce(f32[1024]{0:T(1024)S(1)} %fusion.14, f32[1024]{0:T(1024)S(1)} %fusion.19), channel_id=1, replica_groups=mesh['dp'=32,'feat'=4] {'dp'}, use_global_device_ids=true, to_apply=%region_7.0 | all-reduce | flops 2048 | bytes 16384 | tf_op jit(solution)/shard_map/psum | solution.py:27
  200.7 1.6 fusion.9
  202.3 0.0 reduce-scatter.3.cloned.1.call-start
  202.3 58.9 %all-gather.3.cloned.1.call-done = bf16[768,4096]{1,0:T(8,128)(2,1)} async-done(((bf16[768,1024]{1,0:T(8,128)(2,1)}), bf16[768,4096]{1,0:T(8,128)(2,1)}) %all-gather.3.cloned.1.call-update) | async-done | bytes 6291472 | tf_op jit(solution)/shard_map/all_gather | solution.py:38
  261.3 13.0 %fusion.22 = f32[1024,4096]{1,0:T(8,128)} fusion(bf16[768,4096]{1,0:T(8,128)(2,1)} %all-gather.3.cloned.1.call-done, bf16[768,1024]{1,0:T(8,128)(2,1)S(1)} %copy-done.1, f32[1024]{0:T(1024)S(1)} %add_rsqrt_fusion.1, f32[1024]{0:T(1024)S(1)} %get-tuple-element.19), kind=kOutput, calls=%fused_computation.25 | convolution fusion | flops 6445596672 | bytes 24649728 | tf_op jit(solution)/shard_map/dot_general | solution.py:46
  274.3 0.0 all-gather.5.cloned.1.call-start
  274.4 227.4 %reduce-scatter.3.cloned.1.call-done = f32[32,4096]{1,0:T(8,128)} async-done(((f32[1024,4096]{1,0:T(8,128)}), f32[32,4096]{1,0:T(8,128)}) %reduce-scatter.3.cloned.1.call-update) | async-done | bytes 524304 | tf_op jit(solution)/shard_map/reduce_scatter | solution.py:45
  501.8 2.6 select_convert_fusion
  504.4 0.0 reduce-scatter.5.cloned.1.call-start
  504.4 101.7 %all-gather.5.cloned.1.call-done = bf16[1024,4096]{1,0:T(8,128)(2,1)} async-done(((bf16[32,4096]{1,0:T(8,128)(2,1)}), bf16[1024,4096]{1,0:T(8,128)(2,1)}) %all-gather.5.cloned.1.call-update) | async-done | bytes 8388624 | tf_op jit(solution)/shard_map/all_gather | solution.py:65
  606.1 12.4 %fusion.20 = f32[768,4096]{1,0:T(8,128)} fusion(bf16[1024,4096]{1,0:T(8,128)(2,1)} %all-gather.5.cloned.1.call-done, bf16[768,1024]{1,0:T(8,128)(2,1)S(1)} %copy-done.1, f32[1024]{0:T(1024)S(1)} %add_rsqrt_fusion.1, f32[1024]{0:T(1024)S(1)} %get-tuple-element.19), kind=kOutput, calls=%fused_computation.24 | convolution fusion | flops 6445596672 | bytes 22552576 | tf_op jit(solution)/shard_map/dot_general | solution.py:69
  618.5 64.7 %psum.67 = f32[]{:T(128)} all-reduce(f32[]{:T(128)} %get-tuple-element.16), channel_id=1, replica_groups=mesh['dp'=32,'feat'=4] {'dp','feat'}, use_global_device_ids=true, to_apply=%region_10.11 | all-reduce | flops 1 | bytes 8 | tf_op jit(solution)/shard_map/psum | solution.py:61
  683.2 12.4 %fusion.25 = (f32[1024]{0:T(1024)S(1)}, f32[1024]{0:T(1024)S(1)}, f32[768,1024]{1,0:T(8,128)}) fusion(f32[1024]{0:T(1024)S(1)} %add_rsqrt_fusion.1, f32[1024]{0:T(1024)S(1)} %get-tuple-element.19, bf16[768,1024]{1,0:T(8,128)(2,1)S(1)} %copy-done.1, bf16[768,4096]{1,0:T(8,128)(2,1)} %all-gather.3.cloned.1.call-done, ...), kind=kOutput, calls=%fused_computation.39 | convolution fusion | flops 6447167488 | bytes 19415040 | tf_op jit(solution)/shard_map/dot_general | solution.py:66
  695.6 35.4 %reduce-scatter.5.cloned.1.call-done = f32[768,1024]{1,0:T(8,128)} async-done(((f32[768,4096]{1,0:T(8,128)}), f32[768,1024]{1,0:T(8,128)}) %reduce-scatter.5.cloned.1.call-update) | async-done | bytes 3145744 | tf_op jit(solution)/shard_map/reduce_scatter | solution.py:70
  730.9 2.6 fusion.24
  733.5 183.1 %all-reduce = (f32[1024]{0:T(1024)S(1)}, f32[1024]{0:T(1024)S(1)}, f32[1024]{0:T(1024)S(1)}, f32[1024]{0:T(1024)S(1)}) all-reduce(f32[1024]{0:T(1024)S(1)} %get-tuple-element.6, f32[1024]{0:T(1024)S(1)} %get-tuple-element.5, f32[1024]{0:T(1024)S(1)} %get-tuple-element.4, ...), channel_id=1, replica_groups=mesh['dp'=32,'feat'=4] {'dp'}, use_global_device_ids=true, to_apply=%region_14.15 | all-reduce | flops 4096 | bytes 32768 | tf_op jit(solution)/shard_map/psum | solution.py:71
  916.6 4.0 fusion.18
  920.6 1.9 fusion.13
  (18 shorter events, 0.1 us)
Async XLA Ops:
  7.2 102.6 %copy-start = (bf16[768,1024]{1,0:T(8,128)(2,1)S(1)}, bf16[768,1024]{1,0:T(8,128)(2,1)}, u32[]{:S(2)}) copy-start(bf16[768,1024]{1,0:T(8,128)(2,1)} %param.3) | copy-start | bytes 4718596
  7.2 103.1 %copy-start.1 = (bf16[768,1024]{1,0:T(8,128)(2,1)S(1)}, bf16[768,1024]{1,0:T(8,128)(2,1)}, u32[]{:S(2)}) copy-start(bf16[768,1024]{1,0:T(8,128)(2,1)} %param.2) | copy-start | bytes 4718596
  7.2 254.1 %all-gather.3.cloned.1.call-start = ((), (), s32[]{:S(2)}) async-start(), calls=%async_computation.2 | async-start | bytes 7864320 | tf_op jit(solution)/shard_map/all_gather | solution.py:38
  202.3 299.5 %reduce-scatter.3.cloned.1.call-start = ((), (), s32[]{:S(2)}) async-start(), calls=%async_computation.3 | async-start | bytes 17301504 | tf_op jit(solution)/shard_map/reduce_scatter | solution.py:45
  274.3 331.8 %all-gather.5.cloned.1.call-start = ((), (), s32[]{:S(2)}) async-start(), calls=%async_computation.4 | async-start | bytes 8650752 | tf_op jit(solution)/shard_map/all_gather | solution.py:65
  504.4 226.5 %reduce-scatter.5.cloned.1.call-start = ((), (), s32[]{:S(2)}) async-start(), calls=%async_computation.5 | async-start | bytes 15728640 | tf_op jit(solution)/shard_map/reduce_scatter | solution.py:70
  916.6 4.0 copy-start.2
Sparse Core Ops, SparseCore 0:
  202.4 58.8 all-gather.2
  274.4 227.2 reduce-scatter.2
  505.5 100.5 all-gather.4
  618.6 112.2 reduce-scatter.4
where the time goes:
time: 929 us
  blocking collectives  437 us (47%)
  waiting for transfers between devices  423 us (46%)
  matrix products  37.8 us (4%)
  other arithmetic  17.1 us (2%)
  between operations  13.9 us (1%)
    reduce_scatter x1, waiting for transfers between devices, on_device(): lax.psum_scatter(lax.dot_general(low_a, second_full, (((0,), (0,)), ((),...  227 us
    psum x1, blocking collectives, on_device(): lax.psum((jnp.sum(up_a, axis=0), jnp.sum(up_a * norm_a, axis=0), jnp.sum(...  183 us
    all_gather x1, waiting for transfers between devices, on_device(): gathered = lax.all_gather(slope, 'dp', axis=0, tiled=True)  102 us
    psum x1, blocking collectives, on_device(): lax.psum((jnp.sum(first, axis=0), jnp.sum(second, axis=0)), 'dp')  99 us
    psum x1, blocking collectives, on_device(): lax.psum((jnp.sum(centred_a * centred_a, axis=0), jnp.sum(centred_b * cen...  89.9 us
    psum x1, blocking collectives, on_device(): loss = lax.psum(partial_value, ('dp', 'feat'))  64.7 us
    all_gather x1, waiting for transfers between devices, on_device(): second_full = lax.all_gather(low_b, 'feat', axis=1, tiled=True)  58.9 us
    reduce_scatter x1, waiting for transfers between devices, on_device(): up_b = lax.psum_scatter(part_b, 'feat', scatter_dimension=1, tiled=True)  35.4 us
  transfers between devices with their start and end apart: 4, of which 4 were waited for; matrix products, arithmetic and copies ran while one was open for 1% of the time, Pallas kernels for 0%

commit v1 on v0

--- a/solution.py
+++ b/solution.py
@@ -62,7 +62,9 @@
     slope = jnp.where(on_diagonal, -2.0 * (1.0 - corr_tile), 2.0 * off_weight * corr_tile).astype(
         jnp.bfloat16
     )
-    gathered = lax.all_gather(slope, "dp", axis=0, tiled=True)
+    gathered = jnp.concatenate(
+        lax.all_to_all(jnp.stack([slope] * lax.axis_size("dp")), "dp", 0, 0), axis=0
+    )
     up_a = lax.dot_general(
         second_full, gathered, (((1,), (1,)), ((), ())), preferred_element_type=jnp.float32
     )

time: 929 us -> 911 us (0.981)
  waiting for transfers between devices: 423 us -> 332 us
  blocking collectives: 437 us -> 510 us
    all_gather x1 -> x0, waiting for transfers between devices: 102 us -> none  [on_device(): gathered = lax.all_gather(slope, 'dp', axis=0, tiled=True)]
    all_to_all x0 -> x1, blocking collectives: none -> 73.5 us  [on_device(): lax.all_to_all(jnp.stack([slope] * lax.axis_size('dp')), 'dp', 0, 0)]
  transfers between devices with their start and end apart: 4 -> 3, of which waited for: 4 -> 3; matrix products, arithmetic and copies ran while one was open for 1% -> 1% of each run, Pallas kernels for 0% -> 0%
where the time goes in v1:
time: 911 us
  blocking collectives  510 us (56%)
  waiting for transfers between devices  332 us (36%)
  matrix products  34.6 us (4%)
  other arithmetic  16.4 us (2%)
  between operations  13.8 us (2%)
    reduce_scatter x1, waiting for transfers between devices, on_device(): lax.psum_scatter(lax.dot_general(low_a, second_full, (((0,), (0,)), ((),...  236 us
    psum x1, blocking collectives, on_device(): lax.psum((jnp.sum(up_a, axis=0), jnp.sum(up_a * norm_a, axis=0), jnp.sum(...  183 us
    psum x1, blocking collectives, on_device(): lax.psum((jnp.sum(first, axis=0), jnp.sum(second, axis=0)), 'dp')  99 us
    psum x1, blocking collectives, on_device(): lax.psum((jnp.sum(centred_a * centred_a, axis=0), jnp.sum(centred_b * cen...  89.9 us
    all_to_all x1, blocking collectives, on_device(): lax.all_to_all(jnp.stack([slope] * lax.axis_size('dp')), 'dp', 0, 0)  73.5 us
    psum x1, blocking collectives, on_device(): loss = lax.psum(partial_value, ('dp', 'feat'))  64.1 us
    all_gather x1, waiting for transfers between devices, on_device(): second_full = lax.all_gather(low_b, 'feat', axis=1, tiled=True)  58.9 us
    reduce_scatter x1, waiting for transfers between devices, on_device(): up_b = lax.psum_scatter(part_b, 'feat', scatter_dimension=1, tiled=True)  36.8 us
  transfers between devices with their start and end apart: 3, of which 3 were waited for; matrix products, arithmetic and copies ran while one was open for 1% of the time, Pallas kernels for 0%

profile of v1, /device:TPU:0, one launch (start us, length us, event | category | flops | bytes accessed | tf_op | source)
XLA Modules:
  0.0 910.8 jit_solution(17329129606483013691)
XLA Ops:
  7.2 1.8 convert_reduce_fusion
  9.1 1.7 convert_reduce_fusion.1
  10.7 99.0 %all-reduce.2 = (f32[1024]{0:T(1024)S(1)}, f32[1024]{0:T(1024)S(1)}) all-reduce(f32[1024]{0:T(1024)S(1)} %convert_reduce_fusion, f32[1024]{0:T(1024)S(1)} %convert_reduce_fusion.1), channel_id=1, replica_groups=mesh['dp'=32,'feat'=4] {'dp'}, use_global_device_ids=true, to_apply=%region_5.0 | all-reduce | flops 2048 | bytes 16384 | tf_op jit(solution)/shard_map/psum | solution.py:24
  109.8 0.5 fusion.14
  110.3 0.5 fusion.19
  110.7 89.9 %all-reduce.1 = (f32[1024]{0:T(1024)S(1)}, f32[1024]{0:T(1024)S(1)}) all-reduce(f32[1024]{0:T(1024)S(1)} %fusion.14, f32[1024]{0:T(1024)S(1)} %fusion.19), channel_id=1, replica_groups=mesh['dp'=32,'feat'=4] {'dp'}, use_global_device_ids=true, to_apply=%region_7.0 | all-reduce | flops 2048 | bytes 16384 | tf_op jit(solution)/shard_map/psum | solution.py:27
  200.7 1.6 fusion.9
  202.3 0.0 reduce-scatter.3.cloned.1.call-start
  202.3 58.9 %all-gather.2.cloned.1.call-done = bf16[768,4096]{1,0:T(8,128)(2,1)} async-done(((bf16[768,1024]{1,0:T(8,128)(2,1)}), bf16[768,4096]{1,0:T(8,128)(2,1)}) %all-gather.2.cloned.1.call-update) | async-done | bytes 6291472 | tf_op jit(solution)/shard_map/all_gather | solution.py:38
  261.3 13.0 %fusion.22 = f32[1024,4096]{1,0:T(8,128)} fusion(bf16[768,4096]{1,0:T(8,128)(2,1)} %all-gather.2.cloned.1.call-done, bf16[768,1024]{1,0:T(8,128)(2,1)S(1)} %copy-done.1, f32[1024]{0:T(1024)S(1)} %add_rsqrt_fusion.1, f32[1024]{0:T(1024)S(1)} %get-tuple-element.19), kind=kOutput, calls=%fused_computation.25 | convolution fusion | flops 6445596672 | bytes 24649728 | tf_op jit(solution)/shard_map/dot_general | solution.py:46
  274.3 0.0 reduce-scatter.5.cloned.1.call-start
  274.4 236.0 %reduce-scatter.3.cloned.1.call-done = f32[32,4096]{1,0:T(8,128)} async-done(((f32[1024,4096]{1,0:T(8,128)}), f32[32,4096]{1,0:T(8,128)}) %reduce-scatter.3.cloned.1.call-update) | async-done | bytes 524304 | tf_op jit(solution)/shard_map/reduce_scatter | solution.py:45
  510.4 1.9 select_convert_fusion
  512.3 1.0 stack.2
  513.3 73.5 %all_to_all.5 = bf16[32,32,4096]{2,1,0:T(8,128)(2,1)S(1)} all-to-all(bf16[32,32,4096]{2,1,0:T(8,128)(2,1)S(1)} %stack.2), channel_id=1, replica_groups=mesh['dp'=32,'feat'=4] {'dp'}, dimensions={0} | all-to-all | bytes 16777216 | tf_op jit(solution)/shard_map/all_to_all | solution.py:66
  586.8 3.2 copy-done.3
  590.0 9.2 %fusion.20 = f32[768,4096]{1,0:T(8,128)} fusion(bf16[1024,4096]{1,0:T(8,128)(2,1)S(1)} %bitcast.5, bf16[768,1024]{1,0:T(8,128)(2,1)S(1)} %copy-done.1, f32[1024]{0:T(1024)S(1)} %add_rsqrt_fusion.1, f32[1024]{0:T(1024)S(1)} %get-tuple-element.19), kind=kOutput, calls=%fused_computation.24 | convolution fusion | flops 6445596672 | bytes 22552576 | tf_op jit(solution)/shard_map/dot_general | solution.py:71
  599.2 64.1 %psum.67 = f32[]{:T(128)} all-reduce(f32[]{:T(128)} %get-tuple-element.16), channel_id=1, replica_groups=mesh['dp'=32,'feat'=4] {'dp','feat'}, use_global_device_ids=true, to_apply=%region_10.11 | all-reduce | flops 1 | bytes 8 | tf_op jit(solution)/shard_map/psum | solution.py:61
  663.3 12.4 %fusion.25 = (f32[1024]{0:T(1024)S(1)}, f32[1024]{0:T(1024)S(1)}, f32[768,1024]{1,0:T(8,128)}) fusion(f32[1024]{0:T(1024)S(1)} %add_rsqrt_fusion.1, f32[1024]{0:T(1024)S(1)} %get-tuple-element.19, bf16[768,1024]{1,0:T(8,128)(2,1)S(1)} %copy-done.1, bf16[768,4096]{1,0:T(8,128)(2,1)} %all-gather.2.cloned.1.call-done, bf16[1024,4096]{1,0:T(8,128)(2,1)} %bitcast.6), kind=kOutput, calls=%fused_computation.39 | convolution fusion | flops 6447167488 | bytes 19415040 | tf_op jit(solution)/shard_map/dot_general | solution.py:68
  675.7 36.8 %reduce-scatter.5.cloned.1.call-done = f32[768,1024]{1,0:T(8,128)} async-done(((f32[768,4096]{1,0:T(8,128)}), f32[768,1024]{1,0:T(8,128)}) %reduce-scatter.5.cloned.1.call-update) | async-done | bytes 3145744 | tf_op jit(solution)/shard_map/reduce_scatter | solution.py:72
  712.5 2.6 fusion.24
  715.1 183.2 %all-reduce = (f32[1024]{0:T(1024)S(1)}, f32[1024]{0:T(1024)S(1)}, f32[1024]{0:T(1024)S(1)}, f32[1024]{0:T(1024)S(1)}) all-reduce(f32[1024]{0:T(1024)S(1)} %get-tuple-element.6, f32[1024]{0:T(1024)S(1)} %get-tuple-element.5, f32[1024]{0:T(1024)S(1)} %get-tuple-element.4, ...), channel_id=1, replica_groups=mesh['dp'=32,'feat'=4] {'dp'}, use_global_device_ids=true, to_apply=%region_14.15 | all-reduce | flops 4096 | bytes 32768 | tf_op jit(solution)/shard_map/psum | solution.py:73
  898.4 4.0 fusion.18
  902.3 1.9 fusion.13
  (19 shorter events, 0.1 us)
Async XLA Ops:
  7.2 102.6 %copy-start = (bf16[768,1024]{1,0:T(8,128)(2,1)S(1)}, bf16[768,1024]{1,0:T(8,128)(2,1)}, u32[]{:S(2)}) copy-start(bf16[768,1024]{1,0:T(8,128)(2,1)} %param.3) | copy-start | bytes 4718596
  7.2 103.1 %copy-start.1 = (bf16[768,1024]{1,0:T(8,128)(2,1)S(1)}, bf16[768,1024]{1,0:T(8,128)(2,1)}, u32[]{:S(2)}) copy-start(bf16[768,1024]{1,0:T(8,128)(2,1)} %param.2) | copy-start | bytes 4718596
  7.2 254.1 %all-gather.2.cloned.1.call-start = ((), (), s32[]{:S(2)}) async-start(), calls=%async_computation.3 | async-start | bytes 7864320 | tf_op jit(solution)/shard_map/all_gather | solution.py:38
  202.3 308.1 %reduce-scatter.3.cloned.1.call-start = ((), (), s32[]{:S(2)}) async-start(), calls=%async_computation.4 | async-start | bytes 17301504 | tf_op jit(solution)/shard_map/reduce_scatter | solution.py:45
  274.3 438.2 %reduce-scatter.5.cloned.1.call-start = ((), (), s32[]{:S(2)}) async-start(), calls=%async_computation.5 | async-start | bytes 15728640 | tf_op jit(solution)/shard_map/reduce_scatter | solution.py:72
  586.8 3.2 copy-start.3
  898.3 4.0 copy-start.2
Sparse Core Ops, SparseCore 0:
  202.4 58.8 all-gather.1
  274.4 235.9 reduce-scatter.2
  599.4 113.1 reduce-scatter.4
